TPU v7x, 256 devices: a whole 4x4x8 slice. The times are simulated.
256 devices in a mesh: ia: 4 (over z_lo), ja: 8 (over y, core), ka: 8 (over x, z_hi).
Axes of the slice: x: 4, y: 4, z: 8 (z_hi: 2, z_lo: 4; z = z_hi * 4 + z_lo), core: 2. Of those that a mesh axis runs over, the one named last changes fastest.
Arguments:
- features: bfloat16 [768, 6144], P('ia', ('ka', 'ja')), may hold values from -6 to 6
- in_weight: bfloat16 [6144, 24576], P(('ka', 'ia'), 'ja'), may hold values from -0.078125 to 0.078125
- out_weight: bfloat16 [24576, 6144], P(('ja', 'ia'), 'ka'), may hold values from -0.0390625 to 0.0390625
- cotangent: bfloat16 [768, 6144], P('ia', ('ka', 'ja')), may hold values from -1.5 to 1.5
Outputs:
- layer_out: bfloat16 [768, 6144], P('ia', ('ka', 'ja'))
- feature_grad: bfloat16 [768, 6144], P('ia', ('ka', 'ja'))
- in_weight_grad: bfloat16 [6144, 24576], P(('ka', 'ia'), 'ja')
- out_weight_grad: bfloat16 [24576, 6144], P(('ja', 'ia'), 'ka')
All inputs are finite; a program needn't handle non-finite values.
Results may differ from a plain program's by a relative error of at most 0.028.
Values may be sent and summed in bfloat16 or wider, within the bound.
A program may use at most 64 MiB of HBM per device.

v0:
```python
import jax
import jax.numpy as jnp
from jax import lax
from jax.sharding import PartitionSpec as P

GELU_SCALE = 0.7978845608028654


def gelu_value(hidden):
    inner = GELU_SCALE * (hidden + 0.044715 * hidden * hidden * hidden)
    return 0.5 * hidden * (1.0 + jnp.tanh(inner))


def gelu_slope(hidden):
    tangent = jnp.tanh(GELU_SCALE * (hidden + 0.044715 * hidden * hidden * hidden))
    return 0.5 * (1.0 + tangent) + 0.5 * hidden * (1.0 - tangent * tangent) * GELU_SCALE * (
        1.0 + 3.0 * 0.044715 * hidden * hidden
    )


def transposed(left, right):
    return lax.dot_general(
        left, right, (((1,), (1,)), ((), ())), preferred_element_type=jnp.float32
    )


def inner_rows(left, right):
    return lax.dot_general(
        left, right, (((0,), (0,)), ((), ())), preferred_element_type=jnp.float32
    )


def local(features, in_weight, out_weight, cotangent):
    feature_block = lax.all_gather(features, "ja", axis=1, tiled=True)
    in_full = lax.all_gather(in_weight, "ia", axis=0, tiled=True)
    hidden_part = jnp.dot(feature_block, in_full, preferred_element_type=jnp.float32)
    pre_act = lax.psum_scatter(
        hidden_part.astype(jnp.bfloat16), "ka", scatter_dimension=1, tiled=True
    ).astype(jnp.float32)
    active_local = gelu_value(pre_act).astype(jnp.bfloat16)
    active_block = lax.all_gather(active_local, "ka", axis=1, tiled=True)
    out_full = lax.all_gather(out_weight, "ia", axis=0, tiled=True)
    output_part = jnp.dot(active_block, out_full, preferred_element_type=jnp.float32)
    layer_out = lax.psum_scatter(
        output_part.astype(jnp.bfloat16), "ja", scatter_dimension=1, tiled=True
    )
    cot_block = lax.all_gather(cotangent, "ja", axis=1, tiled=True)
    grad_part = transposed(cot_block, out_full)
    grad_active = lax.psum_scatter(
        grad_part.astype(jnp.bfloat16), "ka", scatter_dimension=1, tiled=True
    ).astype(jnp.float32)
    grad_local = (grad_active * gelu_slope(pre_act)).astype(jnp.bfloat16)
    grad_block = lax.all_gather(grad_local, "ka", axis=1, tiled=True)
    out_weight_grad = lax.psum_scatter(
        inner_rows(active_block, cot_block).astype(jnp.bfloat16),
        "ia",
        scatter_dimension=0,
        tiled=True,
    )
    in_weight_grad = lax.psum_scatter(
        inner_rows(feature_block, grad_block).astype(jnp.bfloat16),
        "ia",
        scatter_dimension=0,
        tiled=True,
    )
    input_part = transposed(grad_block, in_full)
    feature_grad = lax.psum_scatter(
        input_part.astype(jnp.bfloat16), "ja", scatter_dimension=1, tiled=True
    )
    return (layer_out, feature_grad, in_weight_grad, out_weight_grad)


def solution(mesh):
    placed = (
        P("ia", ("ka", "ja")),
        P(("ka", "ia"), "ja"),
        P(("ja", "ia"), "ka"),
        P("ia", ("ka", "ja")),
    )
    return jax.shard_map(
        local,
        mesh=mesh,
        in_specs=placed,
        out_specs=(
            P("ia", ("ka", "ja")),
            P("ia", ("ka", "ja")),
            P(("ka", "ia"), "ja"),
            P(("ja", "ia"), "ka"),
        ),
        check_vma=False,
    )
```

profile of v0, /device:TPU:1, one launch (start us, length us, event | category | flops | bytes accessed | tf_op | source)
XLA Modules:
  0.0 770.0 jit_solution(7024939758362729256)
XLA Ops:
  7.2 0.7 all-gather.5.cloned.1.call-update
  8.0 0.7 all-gather.9.cloned.1.call-update
  8.8 16.1 %all_gather.18 = bf16[192,768]{0,1:T(8,128)(2,1)S(1)} all-gather(bf16[192,96]{0,1:T(8,128)(2,1)S(1)} %copy.9), channel_id=1, replica_groups=mesh['ia'=4,'ja'=8,'ka'=8] {'ja'}, dimensions={1}, use_global_device_ids=true | all-gather | bytes 331776 | tf_op jit(solution)/shard_map/all_gather | solution.py:34
  24.9 81.4 %all-gather.5.cloned.1.call-done = bf16[768,3072]{1,0:T(8,128)(2,1)} async-done(((bf16[192,3072]{1,0:T(8,128)(2,1)}), bf16[768,3072]{1,0:T(8,128)(2,1)}) %all-gather.5.cloned.1.call-update) | async-done | bytes 4718608 | tf_op jit(solution)/shard_map/all_gather | solution.py:35
  106.2 3.5 convolution_convert_fusion.3
  109.7 1.5 copy.12
  111.4 13.8 %all_gather.22 = bf16[192,768]{0,1:T(8,128)(2,1)S(1)} all-gather(bf16[192,96]{0,1:T(8,128)(2,1)S(1)} %copy.10), channel_id=1, replica_groups=mesh['ia'=4,'ja'=8,'ka'=8] {'ja'}, dimensions={1}, use_global_device_ids=true | all-gather | bytes 331776 | tf_op jit(solution)/shard_map/all_gather | solution.py:47
  125.3 75.5 %all-gather.9.cloned.1.call-done = bf16[3072,768]{1,0:T(8,128)(2,1)} async-done(((bf16[768,768]{1,0:T(8,128)(2,1)}), bf16[3072,768]{1,0:T(8,128)(2,1)}) %all-gather.9.cloned.1.call-update) | async-done | bytes 4718608 | tf_op jit(solution)/shard_map/all_gather | solution.py:42
  200.8 4.1 convolution_convert_fusion.2
  204.9 1.6 copy.16
  206.5 87.3 %reduce-scatter.19.cloned.1.call-done = bf16[384,192]{1,0:T(8,128)(2,1)} async-done(((bf16[3072,192]{1,0:T(8,128)(2,1)}), bf16[384,192]{1,0:T(8,128)(2,1)}) %reduce-scatter.19.cloned.1.call-update) | async-done | bytes 147472
  293.8 1.1 copy.13
  294.8 89.3 %reduce-scatter.23.cloned.1.call-done = bf16[384,192]{1,0:T(8,128)(2,1)} async-done(((bf16[3072,192]{1,0:T(8,128)(2,1)}), bf16[384,192]{1,0:T(8,128)(2,1)}) %reduce-scatter.23.cloned.1.call-update) | async-done | bytes 147472
  384.1 1.1 copy.17
  385.2 0.9 fusion.8
  386.2 0.5 all-gather.11.cloned.1.call-update
  386.8 59.9 %all-gather.7.cloned.1.call-done = bf16[192,3072]{1,0:T(8,128)(2,1)} async-done(((bf16[192,384]{1,0:T(8,128)(2,1)}), bf16[192,3072]{1,0:T(8,128)(2,1)}) %all-gather.7.cloned.1.call-update) | async-done | bytes 1179664 | tf_op jit(solution)/shard_map/all_gather | solution.py:41
  446.7 3.8 convolution_convert_fusion.5
  450.5 0.9 copy.14
  451.5 57.4 %all-gather.11.cloned.1.call-done = bf16[192,3072]{1,0:T(8,128)(2,1)} async-done(((bf16[192,384]{1,0:T(8,128)(2,1)}), bf16[192,3072]{1,0:T(8,128)(2,1)}) %all-gather.11.cloned.1.call-update) | async-done | bytes 1179664 | tf_op jit(solution)/shard_map/all_gather | solution.py:53
  508.9 4.5 convolution_convert_fusion.4
  513.4 0.9 copy.18
  514.4 3.6 convolution_convert_fusion
  518.1 1.2 copy-done
  519.3 3.7 fusion
  523.0 6.7 copy.20
  529.7 9.7 %reduce-scatter.21.cloned.1.call-done = bf16[96,192]{1,0:T(8,128)(2,1)} async-done(((bf16[768,192]{1,0:T(8,128)(2,1)}), bf16[96,192]{1,0:T(8,128)(2,1)}) %reduce-scatter.21.cloned.1.call-update) | async-done | bytes 36880
  539.5 1.5 copy.15
  541.0 33.3 %reduce-scatter.25.cloned.1.call-done = bf16[96,192]{1,0:T(8,128)(2,1)} async-done(((bf16[768,192]{1,0:T(8,128)(2,1)}), bf16[96,192]{1,0:T(8,128)(2,1)}) %reduce-scatter.25.cloned.1.call-update) | async-done | bytes 36880
  574.3 1.5 copy.19
  575.8 93.2 %reduce-scatter.17.cloned.1.call-done = bf16[768,768]{1,0:T(8,128)(2,1)} async-done(((bf16[3072,768]{1,0:T(8,128)(2,1)}), bf16[768,768]{1,0:T(8,128)(2,1)}) %reduce-scatter.17.cloned.1.call-update) | async-done | bytes 1179664 | tf_op jit(solution)/shard_map/reduce_scatter | solution.py:54
  669.0 94.2 %reduce-scatter.27.cloned.1.call-done = bf16[192,3072]{1,0:T(8,128)(2,1)} async-done(((bf16[768,3072]{1,0:T(8,128)(2,1)}), bf16[192,3072]{1,0:T(8,128)(2,1)}) %reduce-scatter.27.cloned.1.call-update) | async-done | bytes 1179664
  (26 shorter events, 0.7 us)
Async XLA Ops:
  7.2 1.5 copy-start.2
  7.2 99.1 %all-gather.5.cloned.1.call-start = ((), (), s32[]{:S(2)}) async-start(), calls=%async_computation.6 | async-start | bytes 5898240 | tf_op jit(solution)/shard_map/all_gather | solution.py:35
  7.9 192.9 %all-gather.9.cloned.1.call-start = ((), (), s32[]{:S(2)}) async-start(), calls=%async_computation.8 | async-start | bytes 5898240 | tf_op jit(solution)/shard_map/all_gather | solution.py:42
  8.7 285.1 %reduce-scatter.19.cloned.1.call-start = ((), (), s32[]{:S(2)}) async-start(), calls=%async_computation.11 | async-start | bytes 1769472
  109.7 1.6 copy-start.3
  111.3 272.8 %reduce-scatter.23.cloned.1.call-start = ((), (), s32[]{:S(2)}) async-start(), calls=%async_computation.13 | async-start | bytes 1769472
  206.4 240.3 %all-gather.7.cloned.1.call-start = ((), (), s32[]{:S(2)}) async-start(), calls=%async_computation.7 | async-start | bytes 1327104 | tf_op jit(solution)/shard_map/all_gather | solution.py:41
  386.1 122.7 %all-gather.11.cloned.1.call-start = ((), (), s32[]{:S(2)}) async-start(), calls=%async_computation.9 | async-start | bytes 1327104 | tf_op jit(solution)/shard_map/all_gather | solution.py:53
  386.7 152.7 %reduce-scatter.21.cloned.1.call-start = ((), (), s32[]{:S(2)}) async-start(), calls=%async_computation.12 | async-start | bytes 442368
  451.4 122.8 %reduce-scatter.25.cloned.1.call-start = ((), (), s32[]{:S(2)}) async-start(), calls=%async_computation.14 | async-start | bytes 442368
  508.9 5.5 copy-start.1
  514.3 154.7 %reduce-scatter.17.cloned.1.call-start = ((), (), s32[]{:S(2)}) async-start(), calls=%async_computation.10 | async-start | bytes 5898240 | tf_op jit(solution)/shard_map/reduce_scatter | solution.py:54
  518.0 1.3 copy-start
  518.0 245.2 %reduce-scatter.27.cloned.1.call-start = ((), (), s32[]{:S(2)}) async-start(), calls=%async_computation.15 | async-start | bytes 5898240
Sparse Core Ops, SparseCore 0:
  9.8 96.3 all-gather.4
  108.0 92.6 all-gather.8
  204.8 88.8 reduce-scatter.18
  297.7 86.4 reduce-scatter.22
  387.0 59.6 all-gather.6
  449.6 59.2 all-gather.10
  511.4 28.0 reduce-scatter.20
  542.1 32.0 reduce-scatter.24
  577.4 91.5 reduce-scatter.16
  672.0 91.1 reduce-scatter.26
where the time goes:
time: 771 us; the launch traced here: 770 us
  waiting for transfers between devices  683 us (89%)
  blocking collectives  29.9 us (4%)
  matrix products  23.1 us (3%)
  local copies, waits for them, and re-layouts  18.2 us (2%)
  between operations  14.3 us (2%)
    unnamed x15, waiting for transfers between devices  316 us
    reduce_scatter x1, waiting for transfers between devices, local(): lax.psum_scatter(inner_rows(active_block, cot_block).astype(jnp.bfloat16)...  93.2 us
    all_gather x1, waiting for transfers between devices, local(): in_full = lax.all_gather(in_weight, 'ia', axis=0, tiled=True)  81.4 us
    all_gather x1, waiting for transfers between devices, local(): out_full = lax.all_gather(out_weight, 'ia', axis=0, tiled=True)  75.5 us
    all_gather x1, waiting for transfers between devices, local(): active_block = lax.all_gather(active_local, 'ka', axis=1, tiled=True)  59.9 us
    all_gather x1, waiting for transfers between devices, local(): grad_block = lax.all_gather(grad_local, 'ka', axis=1, tiled=True)  57.4 us
    unnamed x19, local copies, waits for them, and re-layouts  18.2 us
    all_gather x1, blocking collectives, local(): feature_block = lax.all_gather(features, 'ja', axis=1, tiled=True)  16.1 us
  transfers between devices with their start and end apart: 10, of which 10 were waited for; matrix products, arithmetic and copies ran while one was open for 5% of the time, Pallas kernels for 0%

commit v1 on v0

v1 whole, which is shorter than its diff:
```python
import functools

import jax
import jax.numpy as jnp
from jax import lax
from jax.experimental import pallas as pl
from jax.experimental.pallas import tpu as pltpu
from jax.sharding import PartitionSpec as P

GELU_SCALE = 0.7978845608028654
BF = jnp.bfloat16
F32 = jnp.float32
MESH = pl.DeviceIdType.MESH

NI, NY, NC, NX, NZ = 4, 4, 2, 4, 2
NJ = NY * NC
ROWS, FEAT, BLOCK = 192, 96, 768
TOKENS = NI * ROWS
PACK, PR, PW = 4, 48, 384
NH = 3
HC = BLOCK // NH
HALF = ROWS // 2


def dot(left, right, contract):
    return lax.dot_general(left, right, (contract, ((), ())), preferred_element_type=F32)


NN = ((1,), (0,))
NT = ((1,), (1,))
TN = ((0,), (0,))


def kernel(
    feat_ref, cot_ref, w1_ref, w2_hbm,
    out_ref, fgrad_ref, dw1_ref, dw2_ref,
    gx, gc, xs, cs, w1r, w2, gpart, ppart, grecv, precv, gsum, psum, gsend, psend, gz, pz,
    act, gp, dwb, dw2b, pk, rc, s1, ry, s2, rz, send_sem, recv_sem, local_sem,
):
    ia, ja, ka = lax.axis_index("ia"), lax.axis_index("ja"), lax.axis_index("ka")
    yy, cc, xx, zz = ja // NC, lax.rem(ja, NC), ka // NZ, lax.rem(ka, NZ)

    def at_i(d):
        i = lax.rem(ia + d, NI)
        return i, (i, ja, ka)

    def at_y(d):
        y = lax.rem(yy + d, NY)
        return y, (ia, y * NC + cc, ka)

    def at_x(d):
        x = lax.rem(xx + d, NX)
        return x, (ia, ja, x * NZ + zz)

    core = (ia, yy * NC + 1 - cc, ka)
    zpair = (ia, ja, xx * NZ + 1 - zz)

    barrier = pltpu.get_barrier_semaphore()
    peers = [at_i(d)[1] for d in (1, 2, 3)] + [at_y(d)[1] for d in (1, 2, 3)]
    peers += [at_x(d)[1] for d in (1, 2, 3)] + [core, zpair]
    for peer in peers:
        pl.semaphore_signal(barrier, inc=1, device_id=peer, device_id_type=MESH)

    count = [0, 0]
    sent, local = [], []

    def remote(src, dst, device):
        n = count[0]
        count[0] += 1
        copy = pltpu.make_async_remote_copy(
            src_ref=src, dst_ref=dst, send_sem=send_sem.at[n], recv_sem=recv_sem.at[n],
            device_id=device, device_id_type=MESH,
        )
        copy.start()
        sent.append(copy)
        return copy

    def nearby(src, dst):
        n = count[1]
        count[1] += 1
        copy = pltpu.make_async_copy(src, dst, local_sem.at[n])
        copy.start()
        return copy

    def cols(index, width):
        return pl.ds(pl.multiple_of(index * width, width), width)

    w2_copy = nearby(w2_hbm, w2)
    w1_own = [nearby(w1_ref.at[:, cols(ia * NH + h, HC)], w1r.at[h, cols(ia, ROWS)]) for h in range(NH)]
    gc[ja, ia] = cot_ref[...]
    gx[ja, ia] = feat_ref[...]
    pl.semaphore_wait(barrier, len(peers))

    z_c = [remote(cot_ref, gc.at[ja, ia], at_i(d)[1]) for d in (1, 2, 3)]
    z_x = [remote(feat_ref, gx.at[ja, ia], at_i(d)[1]) for d in (1, 2, 3)]
    y_copies, core_copies = [], []
    for buf, arrivals in ((gc, z_c), (gx, z_x)):
        for copy in arrivals:
            copy.wait_recv()
        y_copies.append([remote(buf.at[ja], buf.at[ja], at_y(d)[1]) for d in (1, 2, 3)])
        core_copies.append([remote(buf.at[ja], buf.at[ja], core)])

    w1_in = []
    for h in range(NH):
        w1_in.append([])
        for d in (1, 2, 3):
            i, device = at_i(d)
            w1_in[h].append(remote(w1_ref.at[:, cols(i * NH + h, HC)], w1r.at[h, cols(ia, ROWS)], device))

    def unpack(buf, dst):
        def body(i, carry):
            for g in range(PACK):
                row = pl.multiple_of(i * ROWS + g * PR, PR)
                dst[pl.ds(row, PR), :] = jnp.concatenate(
                    [buf[j, i, :, g * FEAT:(g + 1) * FEAT] for j in range(NJ)], axis=1
                )
            return carry
        lax.fori_loop(0, NI, body, 0)

    def finish_gather(n, buf, dst):
        for d, copy in zip((1, 2, 3), y_copies[n]):
            copy.wait_recv()
            j = lax.rem(yy + NY - d, NY) * NC + cc
            core_copies[n].append(remote(buf.at[j], buf.at[j], core))
        for copy in core_copies[n]:
            copy.wait_recv()
        unpack(buf, dst)

    finish_gather(0, gc, cs)
    w2_copy.wait()
    for h in range(NH):
        def body(t, carry):
            rows = cols(t, ROWS)
            gpart[h, rows] = dot(cs[rows], w2[h * HC:(h + 1) * HC], NT).astype(BF)
            return carry
        lax.fori_loop(0, NX, body, 0)
    g_x = []
    for d in (1, 2, 3):
        x, device = at_x(d)
        g_x.append(remote(gpart.at[:, cols(x, ROWS)], grecv.at[d - 1], device))

    finish_gather(1, gx, xs)
    p_x = []
    for h in range(NH):
        w1_own[h].wait()
        for copy in w1_in[h]:
            copy.wait_recv()

        def body(t, carry):
            rows = cols(t, ROWS)
            ppart[h, rows] = dot(xs[rows], w1r[h], NN).astype(BF)
            return carry
        lax.fori_loop(0, NX, body, 0)
        p_x.append([])
        for d in (1, 2, 3):
            x, device = at_x(d)
            p_x[h].append(remote(ppart.at[h, cols(x, ROWS)], precv.at[h, d - 1], device))

    for copy in g_x:
        copy.wait_recv()
    for h in range(NH):
        total = gpart[h, cols(xx, ROWS)].astype(F32)
        for d in range(3):
            total += grecv[d, h].astype(F32)
        for half in range(2):
            gsum[half, h] = total[half * HALF:(half + 1) * HALF]
            gsend[half, h] = total[half * HALF:(half + 1) * HALF].astype(BF)
    g_z = remote(gsend.at[1 - zz], gz, zpair)
    p_z = []
    for h in range(NH):
        for copy in p_x[h]:
            copy.wait_recv()
        total = ppart[h, cols(xx, ROWS)].astype(F32)
        for d in range(3):
            total += precv[h, d].astype(F32)
        for half in range(2):
            psum[h, half] = total[half * HALF:(half + 1) * HALF]
            psend[h, half] = total[half * HALF:(half + 1) * HALF].astype(BF)
        p_z.append(remote(psend.at[h, 1 - zz], pz.at[h], zpair))

    g_z.wait_recv()
    mine = pl.ds(pl.multiple_of(xx * ROWS + zz * HALF, HALF), HALF)
    theirs = pl.ds(pl.multiple_of(xx * ROWS + (1 - zz) * HALF, HALF), HALF)
    pair, direct, passed = {}, {}, {}
    for h in range(NH):
        p_z[h].wait_recv()
        pre = psum[h, zz] + pz[h].astype(F32)
        grad = gsum[zz, h] + gz[h].astype(F32)
        square = pre * pre
        tangent = jnp.tanh(GELU_SCALE * (pre + 0.044715 * square * pre))
        act[h, mine] = (0.5 * pre * (1.0 + tangent)).astype(BF)
        slope = 0.5 * (1.0 + tangent) + 0.5 * pre * (1.0 - tangent * tangent) * GELU_SCALE * (
            1.0 + 3.0 * 0.044715 * square
        )
        gp[h, mine] = (grad * slope).astype(BF)
        for n, buf in ((0, gp), (1, act)):
            pair[n, h] = remote(buf.at[h, mine], buf.at[h, mine], zpair)
            direct[n, h] = [remote(buf.at[h, mine], buf.at[h, mine], at_x(d)[1]) for d in (1, 2, 3)]
    for n, buf in ((0, gp), (1, act)):
        for h in range(NH):
            pair[n, h].wait_recv()
            passed[n, h] = [remote(buf.at[h, theirs], buf.at[h, theirs], at_x(d)[1]) for d in (1, 2, 3)]

    dw1_in, dw1_own = [], []
    for h in range(NH):
        for copy in direct[0, h] + passed[0, h]:
            copy.wait_recv()

        def body(t, carry):
            dwb[h, cols(t, 256)] = dot(xs[:, cols(t, 256)], gp[h], TN).astype(BF)
            return carry
        lax.fori_loop(0, BLOCK // 256, body, 0)
        for d in (1, 2, 3):
            i, device = at_i(d)
            dw1_in.append(remote(dwb.at[h, cols(i, ROWS)], dw1_ref.at[:, cols(ia * NH + h, HC)], device))
        dw1_own.append(nearby(dwb.at[h, cols(ia, ROWS)], dw1_ref.at[:, cols(ia * NH + h, HC)]))

    def pack(n, value, i):
        value = value.astype(BF)
        for j in range(NJ):
            pk[n, j, i] = jnp.concatenate(
                [value[g * PR:(g + 1) * PR, j * FEAT:(j + 1) * FEAT] for g in range(PACK)], axis=1
            )

    def body(i, carry):
        rows = cols(i, ROWS)
        total = dot(gp[0, rows], w1r[0], NT)
        for h in range(1, NH):
            total += dot(gp[h, rows], w1r[h], NT)
        pack(0, total, i)
        return carry
    lax.fori_loop(0, NI, body, 0)

    def to_core(n):
        return [
            remote(pk.at[n, y * NC + 1 - cc], rc.at[n, y], core) for y in range(NY)
        ]
    core_in = {0: to_core(0)}
    for h in range(NH):
        for copy in direct[1, h] + passed[1, h]:
            copy.wait_recv()

    def body(i, carry):
        rows = cols(i, ROWS)
        total = dot(act[0, rows], w2[0:HC], NN)
        for h in range(1, NH):
            total += dot(act[h, rows], w2[h * HC:(h + 1) * HC], NN)
        pack(1, total, i)
        return carry
    lax.fori_loop(0, NI, body, 0)
    core_in[1] = to_core(1)

    y_in = {}
    for n in range(2):
        for y in range(NY):
            core_in[n][y].wait_recv()
            s1[n, y] = (pk[n, y * NC + cc].astype(F32) + rc[n, y].astype(F32)).astype(BF)
        y_in[n] = []
        for d in (1, 2, 3):
            y, device = at_y(d)
            y_in[n].append(remote(s1.at[n, y], ry.at[n, d - 1], device))

    for h in range(NH):
        dw2b[h * HC:(h + 1) * HC] = dot(act[h], cs[...], TN).astype(BF)
    dw2_copy = nearby(dw2b, dw2_ref)

    z_in = {}
    for n in range(2):
        for copy in y_in[n]:
            copy.wait_recv()
        total = s1[n, yy].astype(F32)
        for d in range(3):
            total += ry[n, d].astype(F32)
        s2[n] = total.astype(BF)
        z_in[n] = []
        for d in (1, 2, 3):
            i, device = at_i(d)
            z_in[n].append(remote(s2.at[n, i], rz.at[n, d - 1], device))
    for n, ref in ((0, fgrad_ref), (1, out_ref)):
        for copy in z_in[n]:
            copy.wait_recv()
        total = s2[n, ia].astype(F32)
        for d in range(3):
            total += rz[n, d].astype(F32)
        ref[...] = total.astype(BF)

    for copy in dw1_in:
        copy.wait_recv()
    for copy in dw1_own + [dw2_copy]:
        copy.wait()
    for copy in sent:
        copy.wait_send()


def packed(piece):
    return piece.reshape(PACK, PR, FEAT).transpose(1, 0, 2).reshape(PR, PW)


def unpacked(piece):
    return piece.reshape(PR, PACK, FEAT).transpose(1, 0, 2).reshape(ROWS, FEAT)


def local(features, in_weight, out_weight, cotangent):
    vmem = pl.BlockSpec(memory_space=pltpu.VMEM)
    hbm = pl.BlockSpec(memory_space=pl.ANY)
    buf = lambda *shape: pltpu.VMEM(shape, BF)
    wide = lambda *shape: pltpu.VMEM(shape, F32)
    out, fgrad, dw1, dw2 = pl.pallas_call(
        kernel,
        out_shape=(
            jax.ShapeDtypeStruct((PR, PW), BF),
            jax.ShapeDtypeStruct((PR, PW), BF),
            jax.ShapeDtypeStruct((ROWS, NI * BLOCK), BF),
            jax.ShapeDtypeStruct((BLOCK, BLOCK), BF),
        ),
        in_specs=[vmem, vmem, hbm, hbm],
        out_specs=(vmem, vmem, hbm, hbm),
        scratch_shapes=[
            buf(NJ, NI, PR, PW), buf(NJ, NI, PR, PW),
            buf(TOKENS, BLOCK), buf(TOKENS, BLOCK),
            buf(NH, BLOCK, HC), buf(BLOCK, BLOCK),
            buf(NH, TOKENS, HC), buf(NH, TOKENS, HC),
            buf(3, NH, ROWS, HC), buf(NH, 3, ROWS, HC),
            wide(2, NH, HALF, HC), wide(NH, 2, HALF, HC),
            buf(2, NH, HALF, HC), buf(NH, 2, HALF, HC),
            buf(NH, HALF, HC), buf(NH, HALF, HC),
            buf(NH, TOKENS, HC), buf(NH, TOKENS, HC),
            buf(NH, BLOCK, HC), buf(BLOCK, BLOCK),
            buf(2, NJ, NI, PR, PW), buf(2, NY, NI, PR, PW),
            buf(2, NY, NI, PR, PW), buf(2, 3, NI, PR, PW),
            buf(2, NI, PR, PW), buf(2, 3, PR, PW),
            pltpu.SemaphoreType.DMA((128,)),
            pltpu.SemaphoreType.DMA((128,)),
            pltpu.SemaphoreType.DMA((12,)),
        ],
        name="block",
        compiler_params=pltpu.CompilerParams(
            collective_id=0, has_side_effects=True, vmem_limit_bytes=56 * 2**20
        ),
        cost_estimate=pl.CostEstimate(
            flops=12 * BLOCK**3, bytes_accessed=8 * BLOCK * BLOCK, transcendentals=HALF * BLOCK
        ),
    )(packed(features), packed(cotangent), in_weight, out_weight)
    return unpacked(out), unpacked(fgrad), dw1, dw2


def solution(mesh):
    placed = (
        P("ia", ("ka", "ja")),
        P(("ka", "ia"), "ja"),
        P(("ja", "ia"), "ka"),
        P("ia", ("ka", "ja")),
    )
    return jax.shard_map(
        local,
        mesh=mesh,
        in_specs=placed,
        out_specs=(
            P("ia", ("ka", "ja")),
            P("ia", ("ka", "ja")),
            P(("ka", "ia"), "ja"),
            P(("ja", "ia"), "ka"),
        ),
        check_vma=False,
    )
```

time: 771 us -> 124 us (0.16)
  waiting for transfers between devices: 683 us -> 0 us
  Pallas kernels: 0 us -> 114 us
  blocking collectives: 29.9 us -> 0 us
  matrix products: 23.1 us -> 0 us
  between operations: 14.3 us -> 0.66 us
  local copies, waits for them, and re-layouts: 18.2 us -> 9.52 us
    unnamed x15 -> x0, waiting for transfers between devices: 316 us -> none
    all_gather x4 -> x0, waiting for transfers between devices: 274 us -> none  [the longest x1 81.4 us: local(): in_full = lax.all_gather(in_weight, 'ia', axis=0, tiled=True)]
    pallas_call x0 -> x1, Pallas kernels: none -> 114 us  [local(): pl.pallas_call(kernel, out_shape=(jax.ShapeDtypeStruct((PR, PW), BF), jax...]
    reduce_scatter x1 -> x0, waiting for transfers between devices: 93.2 us -> none  [local(): lax.psum_scatter(inner_rows(active_block, cot_block).astype(jnp.bfloat16)...]
    all_gather x2 -> x0, blocking collectives: 29.9 us -> none  [the longest x1 16.1 us: local(): feature_block = lax.all_gather(features, 'ja', axis=1, tiled=True)]
    dot_general x6 -> x0, matrix products: 23.1 us -> none  [the longest x2 8.55 us: transposed(): lax.dot_general(left, right, (((1,), (1,)), ((), ())), preferred_element_...]
    unnamed x19 -> x4, local copies, waits for them, and re-layouts: 18.2 us -> 3.47 us
  transfers between devices with their start and end apart: 10 -> 0, of which waited for: 10 -> 0; matrix products, arithmetic and copies ran while one was open for 5% -> 0% of each run, Pallas kernels for 0% -> 0%
where the time goes in v1:
time: 124 us
  Pallas kernels  114 us (92%)
  local copies, waits for them, and re-layouts  9.52 us (8%)
    pallas_call x1, Pallas kernels, local(): pl.pallas_call(kernel, out_shape=(jax.ShapeDtypeStruct((PR, PW), BF), jax...  114 us
    unnamed x4, local copies, waits for them, and re-layouts  3.47 us
    reshape x4, local copies, waits for them, and re-layouts, packed(): return piece.reshape(PACK, PR, FEAT).transpose(1, 0, 2).reshape(PR, PW)  3.08 us

profile of v1, /device:TPU:1, one launch (start us, length us, event | category | flops | bytes accessed | tf_op | source)
XLA Modules:
  0.0 123.7 jit_solution(4606006715637320835)
XLA Ops:
  0.6 0.8 copy.15
  1.5 0.7 reshape.33.feat_ref
  2.2 0.8 copy.14
  3.0 0.7 reshape.35.cot_ref
  3.7 113.5 %block.1 = (bf16[48,384]{1,0:T(8,128)(2,1)}, bf16[48,384]{1,0:T(8,128)(2,1)}, bf16[192,3072]{1,0:T(8,128)(2,1)}, bf16[768,768]{1,0:T(8,128)(2,1)}) custom-call(bf16[48,384]{1,0:T(8,128)(2,1)} %reshape.33.feat_ref, bf16[48,384]{1,0:T(8,128)(2,1)} %reshape.35.cot_ref, bf16[192,3072]{1,0:T(8,128)(2,1)} %w1_ref.1, bf16[768,768]{1,0:T(8,128)(2,1)} %w2_hbm.1), custom_call_target="tpu_custom_call" | custom-call | flops 5435817984 | bytes 4718592 | tf_op jit(solution)/shard_map/block/pallas_call | solution.py:308
  117.2 0.9 reshape.36
  118.1 0.6 copy.10
  118.7 0.9 reshape.38
  119.6 0.6 copy.11
  120.2 0.0 copy-start
  120.2 2.5 %copy.18 = bf16[192,3072]{1,0:T(8,128)(2,1)} copy(bf16[192,3072]{1,0:T(8,128)(2,1)} %get-tuple-element.18) | data formatting | bytes 2359296
  122.7 0.0 copy-done
  122.7 1.0 copy.19
Async XLA Ops:
  120.2 2.5 %copy-start = (bf16[768,768]{1,0:T(8,128)(2,1)S(1)}, bf16[768,768]{1,0:T(8,128)(2,1)}, u32[]{:S(2)}) copy-start(bf16[768,768]{1,0:T(8,128)(2,1)} %get-tuple-element.19) | copy-start | bytes 3538948

commit v2 on v1

v2 whole, which is shorter than its diff:
```python
import functools

import jax
import jax.numpy as jnp
from jax import lax
from jax.experimental import pallas as pl
from jax.experimental.pallas import tpu as pltpu
from jax.sharding import PartitionSpec as P

GELU_SCALE = 0.7978845608028654
BF = jnp.bfloat16
F32 = jnp.float32
MESH = pl.DeviceIdType.MESH

NI, NY, NC, NX, NZ = 4, 4, 2, 4, 2
NJ = NY * NC
RING = NZ * NI
ROWS, FEAT, BLOCK = 192, 96, 768
TOKENS = NI * ROWS
PACK, PR, PW = 4, 48, 384
NH = 3
HC = BLOCK // NH


def dot(left, right, contract):
    return lax.dot_general(left, right, (contract, ((), ())), preferred_element_type=F32)


NN = ((1,), (0,))
NT = ((1,), (1,))
TN = ((0,), (0,))


def guarded(when, action):
    if when is None:
        action()
    else:
        @pl.when(when)
        def _():
            action()


class Transfer:
    def __init__(self, copy, when, arrives):
        self.copy, self.when, self.arrives = copy, when, arrives

    def start(self):
        guarded(self.when, self.copy.start)

    def wait_send(self):
        guarded(self.when, self.copy.wait_send)

    def wait_recv(self):
        guarded(self.arrives, self.copy.wait_recv)


def kernel(
    feat_hbm, cot_hbm, w1_hbm, w2_hbm,
    out_ref, fgrad_ref, dw1_ref, dw2_ref,
    raw, own, gx, gc, xs, xt, cs, w1, w1r, w2, gpart, grecv, gsum, gz, ppart, precv, psum, pz,
    act, gp, dwb, dw2b,
    pk0, rc0, s0, ry0, t0, rb0, rz0, pk1, rc1, s1, ry1, t1, rz1,
    send_sem, recv_sem, local_sem,
):
    ia, ja, ka = lax.axis_index("ia"), lax.axis_index("ja"), lax.axis_index("ka")
    yy, cc, xx, zz = ja // NC, lax.rem(ja, NC), ka // NZ, lax.rem(ka, NZ)
    ring = zz * NI + ia

    def at_i(d):
        i = lax.rem(ia + d, NI)
        return i, (i, ja, ka)

    def at_z(d):
        z = lax.rem(ring + d, RING)
        return z, (lax.rem(z, NI), ja, xx * NZ + z // NI)

    def at_y(d):
        y = lax.rem(yy + d, NY)
        return y, (ia, y * NC + cc, ka)

    def at_x(d):
        x = lax.rem(xx + d, NX)
        return x, (ia, ja, x * NZ + zz)

    core = (ia, yy * NC + 1 - cc, ka)
    zpair = at_z(NI)[1]

    barrier = pltpu.get_barrier_semaphore()
    peers = [at_z(d)[1] for d in range(1, RING)] + [at_y(d)[1] for d in (1, 2, 3)]
    peers += [at_x(d)[1] for d in (1, 2, 3)] + [core]
    for peer in peers:
        pl.semaphore_signal(barrier, inc=1, device_id=peer, device_id_type=MESH)

    count = [0, 0]
    sent = []

    def remote(src, dst, device, when=None, arrives=None):
        n = count[0]
        count[0] += 1
        copy = Transfer(pltpu.make_async_remote_copy(
            src_ref=src, dst_ref=dst, send_sem=send_sem.at[n], recv_sem=recv_sem.at[n],
            device_id=device, device_id_type=MESH,
        ), when, arrives)
        copy.start()
        sent.append(copy)
        return copy

    def nearby(src, dst):
        n = count[1]
        count[1] += 1
        copy = pltpu.make_async_copy(src, dst, local_sem.at[n])
        copy.start()
        return copy

    def cols(index, width):
        return pl.ds(pl.multiple_of(index * width, width), width)

    raw_copies = [nearby(cot_hbm, raw.at[0]), nearby(feat_hbm, raw.at[1])]
    w1_copy = nearby(w1_hbm, w1)
    w2_copy = nearby(w2_hbm, w2)
    for n in range(2):
        raw_copies[n].wait()
        own[n] = jnp.concatenate([raw[n, g * PR:(g + 1) * PR] for g in range(PACK)], axis=1)
    gc[ja, ia] = own[0]
    gx[ja, zz, ia] = own[1]
    pl.semaphore_wait(barrier, len(peers))

    def split(y):
        return lax.rem(y - ia + NI, NI) == 2

    def high(y, c):
        near = lax.rem(y - ia + NI + 1, NI) - 1
        return lax.rem(ring + RING + near - NI * c * ((near + 1) // 3), RING) // NI

    def in_reach(z, row):
        return lax.rem(z - row + 2 + RING, RING) <= 4

    def to_y(src, dst):
        return [remote(src, dst, at_y(d)[1]) for d in (1, 2, 3)]

    z_c = [remote(own.at[0], gc.at[ja, ia], at_i(d)[1]) for d in (1, 2, 3)]
    c_y = [to_y(own.at[0], gc.at[ja, ia])]
    for d, copy in zip((1, 2, 3), z_c):
        copy.wait_recv()
        i = lax.rem(ia + NI - d, NI)
        c_y.append(to_y(gc.at[ja, i], gc.at[ja, i]))
    c_core = [remote(gc.at[ja], gc.at[ja], core)]
    x_z = []
    for d in range(1, RING):
        z, device = at_z(d)
        source = lax.rem(ring + RING - d, RING)
        x_z.append(remote(
            own.at[1], gx.at[ja, zz, ia], device,
            in_reach(z, zz * NI + yy), in_reach(ring, source // NI * NI + yy),
        ))
    for d in (1, 2, 3):
        for copies in c_y:
            copies[d - 1].wait_recv()
        j = lax.rem(yy + NY - d, NY) * NC + cc
        c_core.append(remote(gc.at[j], gc.at[j], core))

    w1_copy.wait()
    w1_in = []
    for h in range(NH):
        w1_in.append([])
        for d in (1, 7, 6 - 4 * cc):
            z, device = at_z(d)
            place = cols(lax.rem(z, NI) * NH + h, HC)
            w1_in[h].append(remote(w1.at[:, place], w1r.at[h, cols(ia, ROWS)], device))
        w1r[h, cols(ia, ROWS)] = w1[:, cols(ia * NH + h, HC)]

    for copy in x_z:
        copy.wait_recv()
    here = high(yy, cc)
    x_y = to_y(gx.at[ja, here], gx.at[ja, here])
    x_b = []
    for d in (1, 2, 3):
        source = lax.rem(yy + NY - d, NY)
        x_b.append(remote(
            gx.at[ja, 1 - here], gx.at[ja, 1 - here], at_y(d)[1], split(yy), split(source)
        ))
    there = high(yy, 1 - cc)
    x_core = [remote(gx.at[ja, there], gx.at[ja, there], core)]

    def unpack(dst, rows_of):
        def body(i, carry):
            for g in range(PACK):
                row = pl.multiple_of(i * ROWS + g * PR, PR)
                dst[pl.ds(row, PR), :] = jnp.concatenate(
                    [rows_of(j, i)[:, g * FEAT:(g + 1) * FEAT] for j in range(NJ)], axis=1
                )
            return carry
        lax.fori_loop(0, NI, body, 0)

    for copy in c_core:
        copy.wait_recv()
    unpack(cs, lambda j, i: gc[j, i])
    w2_copy.wait()

    def over_x(part, landing, h):
        copies = []
        for d in (1, 2, 3):
            x, device = at_x(d)
            copies.append(remote(part.at[h, cols(x, ROWS)], landing.at[h, d - 1], device))
        return copies

    def grad_part(h):
        def body(t, carry):
            rows = cols(t, ROWS)
            gpart[h, rows] = dot(cs[rows], w2[h * HC:(h + 1) * HC], NT).astype(BF)
            return carry
        lax.fori_loop(0, NX, body, 0)
        return over_x(gpart, grecv, h)

    g_x = [grad_part(0), grad_part(1)]

    for d in (1, 2, 3):
        y = lax.rem(yy + NY - d, NY)
        x_y[d - 1].wait_recv()
        x_b[d - 1].wait_recv()
        there = high(y, 1 - cc)
        j = y * NC + cc
        x_core.append(remote(gx.at[j, there], gx.at[j, there], core))
    for copy in x_core:
        copy.wait_recv()
    unpack(xs, lambda j, i: gx[j, high(j // NC, cc), i])

    p_x = []
    for h in range(NH):
        for copy in w1_in[h]:
            copy.wait_recv()

        def body(t, carry):
            rows = cols(t, ROWS)
            ppart[h, rows] = dot(xs[rows], w1r[h], NN).astype(BF)
            return carry
        lax.fori_loop(0, NX, body, 0)
        p_x.append(over_x(ppart, precv, h))
    g_x.append(grad_part(2))

    def body(t, carry):
        xt[cols(t, 256)] = xs[:, cols(t, 256)].T
        return carry
    lax.fori_loop(0, BLOCK // 256, body, 0)

    mine = cols(xx, ROWS)

    def over_pair(part, landing, copies, total_ref, other, h):
        for copy in copies[h]:
            copy.wait_recv()
        total = part[h, mine].astype(F32)
        for d in range(3):
            total += landing[h, d].astype(F32)
        total_ref[h] = total.astype(BF)
        return remote(total_ref.at[h], other.at[h], zpair)

    g_z = [over_pair(gpart, grecv, g_x, gsum, gz, h) for h in range(2)]

    gp_x, act_x = [], []

    def activate(h, pair):
        pair.wait_recv()
        pre = psum[h].astype(F32) + pz[h].astype(F32)
        square = pre * pre
        tangent = jnp.tanh(GELU_SCALE * (pre + 0.044715 * square * pre))
        act[h, mine] = (0.5 * pre * (1.0 + tangent)).astype(BF)
        slope = 0.5 * (1.0 + tangent) + 0.5 * pre * (1.0 - tangent * tangent) * GELU_SCALE * (
            1.0 + 3.0 * 0.044715 * square
        )
        g_z[h].wait_recv()
        grad = gsum[h].astype(F32) + gz[h].astype(F32)
        gp[h, mine] = (grad * slope).astype(BF)
        gp_x.append([remote(gp.at[h, mine], gp.at[h, mine], at_x(d)[1]) for d in (1, 2, 3)])

    def send_act(h):
        act_x.append([remote(act.at[h, mine], act.at[h, mine], at_x(d)[1]) for d in (1, 2, 3)])

    p_z = [over_pair(ppart, precv, p_x, psum, pz, 0), over_pair(ppart, precv, p_x, psum, pz, 1)]
    activate(0, p_z[0])
    p_z.append(over_pair(ppart, precv, p_x, psum, pz, 2))
    g_z.append(over_pair(gpart, grecv, g_x, gsum, gz, 2))
    activate(1, p_z[1])
    send_act(0)
    activate(2, p_z[2])
    send_act(1)
    send_act(2)

    dw1_in, dw1_own = [], []
    for h in range(NH):
        for copy in gp_x[h]:
            copy.wait_recv()

        def body(t, carry):
            dwb[h, cols(t, 256)] = dot(xt[cols(t, 256)], gp[h], NN).astype(BF)
            return carry
        lax.fori_loop(0, BLOCK // 256, body, 0)
        place = cols(ia * NH + h, HC)
        for d in (1, 7, 2 + 4 * cc):
            z, device = at_z(d)
            dw1_in.append(remote(dwb.at[h, cols(lax.rem(z, NI), ROWS)], dw1_ref.at[:, place], device))
        dw1_own.append(nearby(dwb.at[h, cols(ia, ROWS)], dw1_ref.at[:, place]))

    def packed(value, j):
        return jnp.concatenate(
            [value[g * PR:(g + 1) * PR, j * FEAT:(j + 1) * FEAT] for g in range(PACK)], axis=1
        )

    def body(i, carry):
        rows = cols(i, ROWS)
        left = jnp.concatenate([gp[h, rows] for h in range(NH)], axis=1)
        right = jnp.concatenate([w1r[h] for h in range(NH)], axis=1)
        total = dot(left, right, NT).astype(BF)
        for j in range(NJ):
            pk0[j, i] = packed(total, j)
        return carry
    lax.fori_loop(0, NI, body, 0)
    def to_core(part, landing):
        copies = []
        for d in range(NY):
            y = lax.rem(yy + d, NY)
            copies.append(remote(part.at[y * NC + 1 - cc], landing.at[y], core))
        return copies

    core0 = to_core(pk0, rc0)

    y0, b0 = [], []
    for d in (1, 2, 3, 0):
        y, device = at_y(d)
        core0[d].wait_recv()
        s0[y] = pk0[y * NC + cc]

        @pl.when(jnp.logical_not(split(y)))
        def _():
            s0[y] = (pk0[y * NC + cc].astype(F32) + rc0[y].astype(F32)).astype(BF)
        if d:
            y0.append(remote(s0.at[y], ry0.at[d - 1], device))
            b0.append(remote(rc0.at[y], rb0.at[d - 1], device, split(y), split(yy)))

    for copies in act_x:
        for copy in copies:
            copy.wait_recv()

    def body(i, carry):
        rows = cols(i, ROWS)
        left = jnp.concatenate([act[h, rows] for h in range(NH)], axis=1)
        total = dot(left, w2[...], NN).astype(BF)
        for j in range(NJ):
            pk1[j, i] = packed(total, j)
        return carry
    lax.fori_loop(0, NI, body, 0)
    core1 = to_core(pk1, rc1)
    y1 = []
    for d in (1, 2, 3, 0):
        y, device = at_y(d)
        core1[d].wait_recv()
        s1[y] = (pk1[y * NC + cc].astype(F32) + rc1[y].astype(F32)).astype(BF)
        if d:
            y1.append(remote(s1.at[y], ry1.at[d - 1], device))

    for h in range(NH):
        dw2b[h * HC:(h + 1) * HC] = dot(act[h], cs[...], TN).astype(BF)
    dw2_copy = nearby(dw2b, dw2_ref)

    for copy in y0:
        copy.wait_recv()
    total = s0[yy].astype(F32)
    for d in range(3):
        total += ry0[d].astype(F32)
    t0[1 - here] = jnp.zeros((NI, PR, PW), BF)
    t0[here] = total.astype(BF)

    for copy in b0:
        copy.wait_recv()

    @pl.when(split(yy))
    def _():
        total = rc0[yy].astype(F32)
        for d in range(3):
            total += rb0[d].astype(F32)
        t0[1 - here] = total.astype(BF)

    z0 = []
    for d in range(1, RING):
        z, device = at_z(d)
        source = lax.rem(ring + RING - d, RING)
        z0.append(remote(
            t0.at[z // NI, lax.rem(z, NI)], rz0.at[d - 1], device,
            in_reach(ring, z // NI * NI + yy), in_reach(source, zz * NI + yy),
        ))

    for copy in y1:
        copy.wait_recv()
    total = s1[yy].astype(F32)
    for d in range(3):
        total += ry1[d].astype(F32)
    t1[...] = total.astype(BF)
    z1 = []
    for d in (1, 2, 3):
        i, device = at_i(d)
        z1.append(remote(t1.at[i], rz1.at[d - 1], device))

    def finish(total, ref):
        total = total.astype(BF)
        for g in range(PACK):
            ref[g * PR:(g + 1) * PR, :] = total[:, g * FEAT:(g + 1) * FEAT]

    total = t0[zz, ia].astype(F32)
    for n, copy in enumerate(z0):
        copy.wait_recv()

        @pl.when(jnp.logical_not(copy.arrives))
        def _():
            rz0[n] = jnp.zeros((PR, PW), BF)
        total += rz0[n].astype(F32)
    finish(total, fgrad_ref)

    total = t1[ia].astype(F32)
    for n, copy in enumerate(z1):
        copy.wait_recv()
        total += rz1[n].astype(F32)
    finish(total, out_ref)

    for copy in dw1_in:
        copy.wait_recv()
    for copy in dw1_own + [dw2_copy]:
        copy.wait()
    for copy in sent:
        copy.wait_send()


def handover(*refs):
    sources, targets, staging, sem = refs[:4], refs[4:8], refs[8:12], refs[12]
    pieces = []
    for source, stage, target in zip(sources, staging, targets):
        parts = 4 if source.shape[1] > BLOCK // 2 else 1
        rows = source.shape[0] // parts
        for n in range(parts):
            at = pl.ds(n * rows, rows)
            pieces.append((source.at[at], stage.at[at], target.at[at]))
    loads = [pltpu.make_async_copy(p[0], p[1], sem.at[0, n]) for n, p in enumerate(pieces)]
    stores = [pltpu.make_async_copy(p[1], p[2], sem.at[1, n]) for n, p in enumerate(pieces)]
    for load in loads:
        load.start()
    for load, store in zip(loads, stores):
        load.wait()
        store.start()
    for store in stores:
        store.wait()


def local(features, in_weight, out_weight, cotangent):
    vmem = pl.BlockSpec(memory_space=pltpu.VMEM)
    hbm = pl.BlockSpec(memory_space=pl.ANY)
    buf = lambda *shape: pltpu.VMEM(shape, BF)
    wide = lambda *shape: pltpu.VMEM(shape, F32)
    results = pl.pallas_call(
        kernel,
        out_shape=(
            jax.ShapeDtypeStruct((ROWS, FEAT), BF),
            jax.ShapeDtypeStruct((ROWS, FEAT), BF),
            jax.ShapeDtypeStruct((ROWS, NI * BLOCK), BF),
            jax.ShapeDtypeStruct((BLOCK, BLOCK), BF),
        ),
        in_specs=[hbm] * 4,
        out_specs=(vmem, vmem, hbm, hbm),
        scratch_shapes=[
            buf(2, ROWS, FEAT), buf(2, PR, PW), buf(NJ, NZ, NI, PR, PW), buf(NJ, NI, PR, PW),
            buf(TOKENS, BLOCK), buf(BLOCK, TOKENS), buf(TOKENS, BLOCK),
            buf(ROWS, NI * BLOCK), buf(NH, BLOCK, HC), buf(BLOCK, BLOCK),
            buf(NH, TOKENS, HC), buf(NH, 3, ROWS, HC), buf(NH, ROWS, HC), buf(NH, ROWS, HC),
            buf(NH, TOKENS, HC), buf(NH, 3, ROWS, HC), buf(NH, ROWS, HC), buf(NH, ROWS, HC),
            buf(NH, TOKENS, HC), buf(NH, TOKENS, HC),
            buf(NH, BLOCK, HC), buf(BLOCK, BLOCK),
            buf(NJ, NI, PR, PW), buf(NY, NI, PR, PW), buf(NY, NI, PR, PW),
            buf(3, NI, PR, PW), buf(NZ, NI, PR, PW), buf(3, NI, PR, PW), buf(RING - 1, PR, PW),
            buf(NJ, NI, PR, PW), buf(NY, NI, PR, PW), buf(NY, NI, PR, PW),
            buf(3, NI, PR, PW), buf(NI, PR, PW), buf(3, PR, PW),
            pltpu.SemaphoreType.DMA((124,)),
            pltpu.SemaphoreType.DMA((124,)),
            pltpu.SemaphoreType.DMA((8,)),
        ],
        name="block",
        compiler_params=pltpu.CompilerParams(
            collective_id=0, has_side_effects=True, vmem_limit_bytes=60 * 2**20
        ),
        cost_estimate=pl.CostEstimate(
            flops=12 * BLOCK**3, bytes_accessed=8 * BLOCK * BLOCK, transcendentals=ROWS * BLOCK
        ),
    )(features, cotangent, in_weight, out_weight)
    return pl.pallas_call(
        handover,
        out_shape=tuple(jax.ShapeDtypeStruct(r.shape, r.dtype) for r in results),
        in_specs=[hbm] * 4,
        out_specs=(hbm,) * 4,
        scratch_shapes=[pltpu.VMEM(r.shape, r.dtype) for r in results] + [pltpu.SemaphoreType.DMA((2, 10))],
        name="handover",
        compiler_params=pltpu.CompilerParams(vmem_limit_bytes=60 * 2**20),
    )(*results)


def solution(mesh):
    placed = (
        P("ia", ("ka", "ja")),
        P(("ka", "ia"), "ja"),
        P(("ja", "ia"), "ka"),
        P("ia", ("ka", "ja")),
    )
    return jax.shard_map(
        local,
        mesh=mesh,
        in_specs=placed,
        out_specs=(
            P("ia", ("ka", "ja")),
            P("ia", ("ka", "ja")),
            P(("ka", "ia"), "ja"),
            P(("ja", "ia"), "ka"),
        ),
        check_vma=False,
    )
```

time: 124 us -> 113 us (0.911)
  the two profiles are of different devices: /device:TPU:1 before, /device:TPU:17 now
where the time goes in v2:
time: 113 us
  Pallas kernels  112 us (99%)
    pallas_call x1, Pallas kernels, local(): pl.pallas_call(kernel, out_shape=(jax.ShapeDtypeStruct((ROWS, FEAT), BF),...  110 us
    pallas_call x1, Pallas kernels, local(): pl.pallas_call(handover, out_shape=tuple((jax.ShapeDtypeStruct(r.shape, r...  2.59 us

profile of v2, /device:TPU:17, one launch (start us, length us, event | category | flops | bytes accessed | tf_op | source)
XLA Modules:
  0.0 113.1 jit_solution(3214622092624399737)
XLA Ops:
  0.6 109.9 %block.1 = (bf16[192,96]{1,0:T(8,128)(2,1)}, bf16[192,96]{1,0:T(8,128)(2,1)}, bf16[192,3072]{1,0:T(8,128)(2,1)}, bf16[768,768]{1,0:T(8,128)(2,1)}) custom-call(bf16[192,96]{1,0:T(8,128)(2,1)} %feat_hbm.1, bf16[192,96]{1,0:T(8,128)(2,1)} %cot_hbm.1, bf16[192,3072]{1,0:T(8,128)(2,1)} %w1_hbm.1, bf16[768,768]{1,0:T(8,128)(2,1)} %w2_hbm.1), custom_call_target="tpu_custom_call" | custom-call | flops 5435817984 | bytes 4718592 | tf_op jit(solution)/shard_map/block/pallas_call | solution.py:456
  110.5 2.6 %handover.1 = (bf16[192,96]{1,0:T(8,128)(2,1)}, bf16[192,96]{1,0:T(8,128)(2,1)}, bf16[192,3072]{1,0:T(8,128)(2,1)}, bf16[768,768]{1,0:T(8,128)(2,1)}) custom-call(bf16[192,96]{1,0:T(8,128)(2,1)} %get-tuple-element.8.refs_0_, bf16[192,96]{1,0:T(8,128)(2,1)} %get-tuple-element.9.refs_1_, bf16[192,3072]{1,0:T(8,128)(2,1)} %get-tuple-element.10.refs_2_, ...), custom_call_target="tpu_custom_call" | custom-call | tf_op jit(solution)/shard_map/handover/pallas_call | solution.py:490

commit v3 on v2

--- a/solution.py
+++ b/solution.py
@@ -57,9 +57,10 @@
 def kernel(
     feat_hbm, cot_hbm, w1_hbm, w2_hbm,
     out_ref, fgrad_ref, dw1_ref, dw2_ref,
-    raw, own, gx, gc, xs, xt, cs, w1, w1r, w2, gpart, grecv, gsum, gz, ppart, precv, psum, pz,
+    raw, own, gx, gc, xs, xt, cs, w1, w1r, w2, gpart, grecv, gpass, gsum, gz,
+    ppart, precv, ppass, psum, pz,
     act, gp, dwb, dw2b,
-    pk0, rc0, s0, ry0, t0, rb0, rz0, pk1, rc1, s1, ry1, t1, rz1,
+    pk0, rc0, s0, ry0, t0, rz0, pk1, rc1, s1, ry1, t1, rz1,
     send_sem, recv_sem, local_sem,
 ):
     ia, ja, ka = lax.axis_index("ia"), lax.axis_index("ja"), lax.axis_index("ka")
@@ -78,16 +79,19 @@
         y = lax.rem(yy + d, NY)
         return y, (ia, y * NC + cc, ka)
 
-    def at_x(d):
-        x = lax.rem(xx + d, NX)
-        return x, (ia, ja, x * NZ + zz)
+    def at_x(x):
+        return (ia, ja, x * NZ + zz)
+
+    even, odd = xx + 1 - 2 * lax.rem(xx, 2), NX - 1 - xx
+    first, second = even + cc * (odd - even), odd + cc * (even - odd)
+    across = lax.rem(xx + 2, NX)
 
     core = (ia, yy * NC + 1 - cc, ka)
     zpair = at_z(NI)[1]
 
     barrier = pltpu.get_barrier_semaphore()
     peers = [at_z(d)[1] for d in range(1, RING)] + [at_y(d)[1] for d in (1, 2, 3)]
-    peers += [at_x(d)[1] for d in (1, 2, 3)] + [core]
+    peers += [at_x(first), at_x(second), core]
     for peer in peers:
         pl.semaphore_signal(barrier, inc=1, device_id=peer, device_id_type=MESH)
 
@@ -125,15 +129,14 @@
     gx[ja, zz, ia] = own[1]
     pl.semaphore_wait(barrier, len(peers))
 
-    def split(y):
-        return lax.rem(y - ia + NI, NI) == 2
-
-    def high(y, c):
+    odd_z = lax.rem(ia, 2)
+
+    def high(y):
         near = lax.rem(y - ia + NI + 1, NI) - 1
-        return lax.rem(ring + RING + near - NI * c * ((near + 1) // 3), RING) // NI
+        return lax.rem(ring + RING + near - NI * odd_z * ((near + 1) // 3), RING) // NI
 
     def in_reach(z, row):
-        return lax.rem(z - row + 2 + RING, RING) <= 4
+        return lax.rem(row - z + 1 + lax.rem(z, 2) + RING, RING) <= 3
 
     def to_y(src, dst):
         return [remote(src, dst, at_y(d)[1]) for d in (1, 2, 3)]
@@ -153,34 +156,27 @@
             own.at[1], gx.at[ja, zz, ia], device,
             in_reach(z, zz * NI + yy), in_reach(ring, source // NI * NI + yy),
         ))
+    w1_copy.wait()
+    w1_in = []
+    for h in range(NH):
+        w1_in.append([])
+        for d in (1, 7, 6 - 4 * odd_z):
+            z, device = at_z(d)
+            place = cols(lax.rem(z, NI) * NH + h, HC)
+            w1_in[h].append(remote(w1.at[:, place], w1r.at[h, cols(ia, ROWS)], device))
+        w1r[h, cols(ia, ROWS)] = w1[:, cols(ia * NH + h, HC)]
+
     for d in (1, 2, 3):
         for copies in c_y:
             copies[d - 1].wait_recv()
         j = lax.rem(yy + NY - d, NY) * NC + cc
         c_core.append(remote(gc.at[j], gc.at[j], core))
 
-    w1_copy.wait()
-    w1_in = []
-    for h in range(NH):
-        w1_in.append([])
-        for d in (1, 7, 6 - 4 * cc):
-            z, device = at_z(d)
-            place = cols(lax.rem(z, NI) * NH + h, HC)
-            w1_in[h].append(remote(w1.at[:, place], w1r.at[h, cols(ia, ROWS)], device))
-        w1r[h, cols(ia, ROWS)] = w1[:, cols(ia * NH + h, HC)]
-
     for copy in x_z:
         copy.wait_recv()
-    here = high(yy, cc)
+    here = high(yy)
     x_y = to_y(gx.at[ja, here], gx.at[ja, here])
-    x_b = []
-    for d in (1, 2, 3):
-        source = lax.rem(yy + NY - d, NY)
-        x_b.append(remote(
-            gx.at[ja, 1 - here], gx.at[ja, 1 - here], at_y(d)[1], split(yy), split(source)
-        ))
-    there = high(yy, 1 - cc)
-    x_core = [remote(gx.at[ja, there], gx.at[ja, there], core)]
+    x_core = [remote(gx.at[ja, here], gx.at[ja, here], core)]
 
     def unpack(dst, rows_of):
         def body(i, carry):
@@ -197,12 +193,25 @@
     unpack(cs, lambda j, i: gc[j, i])
     w2_copy.wait()
 
-    def over_x(part, landing, h):
-        copies = []
-        for d in (1, 2, 3):
-            x, device = at_x(d)
-            copies.append(remote(part.at[h, cols(x, ROWS)], landing.at[h, d - 1], device))
-        return copies
+    mine = cols(xx, ROWS)
+
+    def sum_first(part, landing, h):
+        return [
+            remote(part.at[h, cols(x, ROWS)], landing.at[h, n], at_x(first))
+            for n, x in ((1, across), (0, first))
+        ]
+
+    def sum_second(part, landing, passing, copies, h):
+        copies[0].wait_recv()
+        passing[h] = (part[h, cols(second, ROWS)].astype(F32) + landing[h, 1].astype(F32)).astype(BF)
+        copies.append(remote(passing.at[h], landing.at[h, 2], at_x(second)))
+
+    def sum_pair(part, landing, total_ref, other, copies, h):
+        copies[1].wait_recv()
+        copies[2].wait_recv()
+        total = part[h, mine].astype(F32) + landing[h, 0].astype(F32) + landing[h, 2].astype(F32)
+        total_ref[h] = total.astype(BF)
+        return remote(total_ref.at[h], other.at[h], zpair)
 
     def grad_part(h):
         def body(t, carry):
@@ -210,20 +219,26 @@
             gpart[h, rows] = dot(cs[rows], w2[h * HC:(h + 1) * HC], NT).astype(BF)
             return carry
         lax.fori_loop(0, NX, body, 0)
-        return over_x(gpart, grecv, h)
-
-    g_x = [grad_part(0), grad_part(1)]
+        return sum_first(gpart, grecv, h)
+
+    g_x = [grad_part(h) for h in range(NH)]
+
+    def grad_second(h):
+        sum_second(gpart, grecv, gpass, g_x[h], h)
+
+    def grad_pair(h):
+        return sum_pair(gpart, grecv, gsum, gz, g_x[h], h)
 
     for d in (1, 2, 3):
         y = lax.rem(yy + NY - d, NY)
         x_y[d - 1].wait_recv()
-        x_b[d - 1].wait_recv()
-        there = high(y, 1 - cc)
+        there = high(y)
         j = y * NC + cc
         x_core.append(remote(gx.at[j, there], gx.at[j, there], core))
+    grad_second(0)
     for copy in x_core:
         copy.wait_recv()
-    unpack(xs, lambda j, i: gx[j, high(j // NC, cc), i])
+    unpack(xs, lambda j, i: gx[j, high(j // NC), i])
 
     p_x = []
     for h in range(NH):
@@ -235,31 +250,52 @@
             ppart[h, rows] = dot(xs[rows], w1r[h], NN).astype(BF)
             return carry
         lax.fori_loop(0, NX, body, 0)
-        p_x.append(over_x(ppart, precv, h))
-    g_x.append(grad_part(2))
+        p_x.append(sum_first(ppart, precv, h))
+        if h < 2:
+            grad_second(h + 1)
+    g_z = [grad_pair(h) for h in range(NH)]
 
     def body(t, carry):
         xt[cols(t, 256)] = xs[:, cols(t, 256)].T
         return carry
     lax.fori_loop(0, BLOCK // 256, body, 0)
 
-    mine = cols(xx, ROWS)
-
-    def over_pair(part, landing, copies, total_ref, other, h):
-        for copy in copies[h]:
-            copy.wait_recv()
-        total = part[h, mine].astype(F32)
-        for d in range(3):
-            total += landing[h, d].astype(F32)
-        total_ref[h] = total.astype(BF)
-        return remote(total_ref.at[h], other.at[h], zpair)
-
-    g_z = [over_pair(gpart, grecv, g_x, gsum, gz, h) for h in range(2)]
+    p_z = []
+
+    def pre_second(h):
+        sum_second(ppart, precv, ppass, p_x[h], h)
+
+    def pre_pair(h):
+        p_z.append(sum_pair(ppart, precv, psum, pz, p_x[h], h))
+
+    pre_second(0)
+    pre_second(1)
+    pre_pair(0)
+    pre_second(2)
+    pre_pair(1)
+    pre_pair(2)
+
+    class Gather:
+        def __init__(self, ref, at):
+            self.ref, self.at = ref, at
+            self.own = [self.send(xx, x) for x in (first, second)]
+
+        def send(self, rows, x):
+            piece = self.ref.at[self.at, cols(rows, ROWS)]
+            return remote(piece, piece, at_x(x))
+
+        def pass_on(self):
+            self.own[0].wait_recv()
+            self.own.append(self.send(first, second))
+
+        def finish(self):
+            for copy in self.own[1:]:
+                copy.wait_recv()
 
     gp_x, act_x = [], []
 
-    def activate(h, pair):
-        pair.wait_recv()
+    def activate(h):
+        p_z[h].wait_recv()
         pre = psum[h].astype(F32) + pz[h].astype(F32)
         square = pre * pre
         tangent = jnp.tanh(GELU_SCALE * (pre + 0.044715 * square * pre))
@@ -270,35 +306,36 @@
         g_z[h].wait_recv()
         grad = gsum[h].astype(F32) + gz[h].astype(F32)
         gp[h, mine] = (grad * slope).astype(BF)
-        gp_x.append([remote(gp.at[h, mine], gp.at[h, mine], at_x(d)[1]) for d in (1, 2, 3)])
-
-    def send_act(h):
-        act_x.append([remote(act.at[h, mine], act.at[h, mine], at_x(d)[1]) for d in (1, 2, 3)])
-
-    p_z = [over_pair(ppart, precv, p_x, psum, pz, 0), over_pair(ppart, precv, p_x, psum, pz, 1)]
-    activate(0, p_z[0])
-    p_z.append(over_pair(ppart, precv, p_x, psum, pz, 2))
-    g_z.append(over_pair(gpart, grecv, g_x, gsum, gz, 2))
-    activate(1, p_z[1])
-    send_act(0)
-    activate(2, p_z[2])
-    send_act(1)
-    send_act(2)
+        gp_x.append(Gather(gp, h))
 
     dw1_in, dw1_own = [], []
-    for h in range(NH):
-        for copy in gp_x[h]:
-            copy.wait_recv()
-
+
+    def in_weight_grad(h):
         def body(t, carry):
             dwb[h, cols(t, 256)] = dot(xt[cols(t, 256)], gp[h], NN).astype(BF)
             return carry
         lax.fori_loop(0, BLOCK // 256, body, 0)
         place = cols(ia * NH + h, HC)
-        for d in (1, 7, 2 + 4 * cc):
+        for d in (1, 7, 2 + 4 * odd_z):
             z, device = at_z(d)
             dw1_in.append(remote(dwb.at[h, cols(lax.rem(z, NI), ROWS)], dw1_ref.at[:, place], device))
         dw1_own.append(nearby(dwb.at[h, cols(ia, ROWS)], dw1_ref.at[:, place]))
+
+    activate(0)
+    activate(1)
+    gp_x[0].pass_on()
+    activate(2)
+    gp_x[1].pass_on()
+    act_x += [Gather(act, 0), Gather(act, 1)]
+    gp_x[2].pass_on()
+    act_x.append(Gather(act, 2))
+    act_x[0].pass_on()
+    act_x[1].pass_on()
+    gp_x[0].finish()
+    in_weight_grad(0)
+    gp_x[1].finish()
+    gp_x[2].finish()
+    act_x[2].pass_on()
 
     def packed(value, j):
         return jnp.concatenate(
@@ -322,23 +359,22 @@
         return copies
 
     core0 = to_core(pk0, rc0)
-
-    y0, b0 = [], []
-    for d in (1, 2, 3, 0):
-        y, device = at_y(d)
-        core0[d].wait_recv()
-        s0[y] = pk0[y * NC + cc]
-
-        @pl.when(jnp.logical_not(split(y)))
-        def _():
-            s0[y] = (pk0[y * NC + cc].astype(F32) + rc0[y].astype(F32)).astype(BF)
-        if d:
-            y0.append(remote(s0.at[y], ry0.at[d - 1], device))
-            b0.append(remote(rc0.at[y], rb0.at[d - 1], device, split(y), split(yy)))
-
-    for copies in act_x:
-        for copy in copies:
-            copy.wait_recv()
+    in_weight_grad(1)
+
+    def to_rows(partial, arrived, copies, summed, landing):
+        started = []
+        for d in (1, 2, 3, 0):
+            y, device = at_y(d)
+            copies[d].wait_recv()
+            summed[y] = (partial[y * NC + cc].astype(F32) + arrived[y].astype(F32)).astype(BF)
+            if d:
+                started.append(remote(summed.at[y], landing.at[d - 1], device))
+        return started
+
+    y0 = to_rows(pk0, rc0, core0, s0, ry0)
+
+    for gather in act_x:
+        gather.finish()
 
     def body(i, carry):
         rows = cols(i, ROWS)
@@ -349,13 +385,8 @@
         return carry
     lax.fori_loop(0, NI, body, 0)
     core1 = to_core(pk1, rc1)
-    y1 = []
-    for d in (1, 2, 3, 0):
-        y, device = at_y(d)
-        core1[d].wait_recv()
-        s1[y] = (pk1[y * NC + cc].astype(F32) + rc1[y].astype(F32)).astype(BF)
-        if d:
-            y1.append(remote(s1.at[y], ry1.at[d - 1], device))
+    in_weight_grad(2)
+    y1 = to_rows(pk1, rc1, core1, s1, ry1)
 
     for h in range(NH):
         dw2b[h * HC:(h + 1) * HC] = dot(act[h], cs[...], TN).astype(BF)
@@ -366,25 +397,13 @@
     total = s0[yy].astype(F32)
     for d in range(3):
         total += ry0[d].astype(F32)
-    t0[1 - here] = jnp.zeros((NI, PR, PW), BF)
-    t0[here] = total.astype(BF)
-
-    for copy in b0:
-        copy.wait_recv()
-
-    @pl.when(split(yy))
-    def _():
-        total = rc0[yy].astype(F32)
-        for d in range(3):
-            total += rb0[d].astype(F32)
-        t0[1 - here] = total.astype(BF)
-
+    t0[...] = total.astype(BF)
     z0 = []
     for d in range(1, RING):
         z, device = at_z(d)
         source = lax.rem(ring + RING - d, RING)
         z0.append(remote(
-            t0.at[z // NI, lax.rem(z, NI)], rz0.at[d - 1], device,
+            t0.at[lax.rem(z, NI)], rz0.at[d - 1], device,
             in_reach(ring, z // NI * NI + yy), in_reach(source, zz * NI + yy),
         ))
 
@@ -404,7 +423,7 @@
         for g in range(PACK):
             ref[g * PR:(g + 1) * PR, :] = total[:, g * FEAT:(g + 1) * FEAT]
 
-    total = t0[zz, ia].astype(F32)
+    total = jnp.where(here == zz, t0[ia].astype(F32), 0.0)
     for n, copy in enumerate(z0):
         copy.wait_recv()
 
@@ -467,16 +486,18 @@
             buf(2, ROWS, FEAT), buf(2, PR, PW), buf(NJ, NZ, NI, PR, PW), buf(NJ, NI, PR, PW),
             buf(TOKENS, BLOCK), buf(BLOCK, TOKENS), buf(TOKENS, BLOCK),
             buf(ROWS, NI * BLOCK), buf(NH, BLOCK, HC), buf(BLOCK, BLOCK),
-            buf(NH, TOKENS, HC), buf(NH, 3, ROWS, HC), buf(NH, ROWS, HC), buf(NH, ROWS, HC),
-            buf(NH, TOKENS, HC), buf(NH, 3, ROWS, HC), buf(NH, ROWS, HC), buf(NH, ROWS, HC),
+            buf(NH, TOKENS, HC), buf(NH, 3, ROWS, HC), buf(NH, ROWS, HC),
+            buf(NH, ROWS, HC), buf(NH, ROWS, HC),
+            buf(NH, TOKENS, HC), buf(NH, 3, ROWS, HC), buf(NH, ROWS, HC),
+            buf(NH, ROWS, HC), buf(NH, ROWS, HC),
             buf(NH, TOKENS, HC), buf(NH, TOKENS, HC),
             buf(NH, BLOCK, HC), buf(BLOCK, BLOCK),
             buf(NJ, NI, PR, PW), buf(NY, NI, PR, PW), buf(NY, NI, PR, PW),
-            buf(3, NI, PR, PW), buf(NZ, NI, PR, PW), buf(3, NI, PR, PW), buf(RING - 1, PR, PW),
+            buf(3, NI, PR, PW), buf(NI, PR, PW), buf(RING - 1, PR, PW),
             buf(NJ, NI, PR, PW), buf(NY, NI, PR, PW), buf(NY, NI, PR, PW),
             buf(3, NI, PR, PW), buf(NI, PR, PW), buf(3, PR, PW),
-            pltpu.SemaphoreType.DMA((124,)),
-            pltpu.SemaphoreType.DMA((124,)),
+            pltpu.SemaphoreType.DMA((118,)),
+            pltpu.SemaphoreType.DMA((118,)),
             pltpu.SemaphoreType.DMA((8,)),
         ],
         name="block",

time: 113 us -> 106 us (0.938)
  the two profiles are of different devices: /device:TPU:17 before, /device:TPU:1 now
where the time goes in v3:
time: 106 us; the launch traced here: 105 us
  Pallas kernels  105 us (99%)
    pallas_call x1, Pallas kernels, local(): pl.pallas_call(kernel, out_shape=(jax.ShapeDtypeStruct((ROWS, FEAT), BF),...  102 us
    pallas_call x1, Pallas kernels, local(): pl.pallas_call(handover, out_shape=tuple((jax.ShapeDtypeStruct(r.shape, r...  2.59 us

profile of v3, /device:TPU:1, one launch (start us, length us, event | category | flops | bytes accessed | tf_op | source)
XLA Modules:
  0.0 105.4 jit_solution(12764284081918212902)
XLA Ops:
  0.6 102.1 %block.1 = (bf16[192,96]{1,0:T(8,128)(2,1)}, bf16[192,96]{1,0:T(8,128)(2,1)}, bf16[192,3072]{1,0:T(8,128)(2,1)}, bf16[768,768]{1,0:T(8,128)(2,1)}) custom-call(bf16[192,96]{1,0:T(8,128)(2,1)} %feat_hbm.1, bf16[192,96]{1,0:T(8,128)(2,1)} %cot_hbm.1, bf16[192,3072]{1,0:T(8,128)(2,1)} %w1_hbm.1, bf16[768,768]{1,0:T(8,128)(2,1)} %w2_hbm.1), custom_call_target="tpu_custom_call" | custom-call | flops 5435817984 | bytes 4718592 | tf_op jit(solution)/shard_map/block/pallas_call | solution.py:475
  102.8 2.6 %handover.1 = (bf16[192,96]{1,0:T(8,128)(2,1)}, bf16[192,96]{1,0:T(8,128)(2,1)}, bf16[192,3072]{1,0:T(8,128)(2,1)}, bf16[768,768]{1,0:T(8,128)(2,1)}) custom-call(bf16[192,96]{1,0:T(8,128)(2,1)} %get-tuple-element.8.refs_0_, bf16[192,96]{1,0:T(8,128)(2,1)} %get-tuple-element.9.refs_1_, bf16[192,3072]{1,0:T(8,128)(2,1)} %get-tuple-element.10.refs_2_, ...), custom_call_target="tpu_custom_call" | custom-call | tf_op jit(solution)/shard_map/handover/pallas_call | solution.py:511

commit v4 on v3

--- a/solution.py
+++ b/solution.py
@@ -388,10 +388,6 @@
     in_weight_grad(2)
     y1 = to_rows(pk1, rc1, core1, s1, ry1)
 
-    for h in range(NH):
-        dw2b[h * HC:(h + 1) * HC] = dot(act[h], cs[...], TN).astype(BF)
-    dw2_copy = nearby(dw2b, dw2_ref)
-
     for copy in y0:
         copy.wait_recv()
     total = s0[yy].astype(F32)
@@ -406,6 +402,10 @@
             t0.at[lax.rem(z, NI)], rz0.at[d - 1], device,
             in_reach(ring, z // NI * NI + yy), in_reach(source, zz * NI + yy),
         ))
+
+    for h in range(NH):
+        dw2b[h * HC:(h + 1) * HC] = dot(act[h], cs[...], TN).astype(BF)
+    dw2_copy = nearby(dw2b, dw2_ref)
 
     for copy in y1:
         copy.wait_recv()

time: 106 us -> 106 us (level)
  no operation moved by 1% of the time
where the time goes in v4:
time: 106 us; the launch traced here: 105 us
  Pallas kernels  105 us (99%)
    pallas_call x1, Pallas kernels, local(): pl.pallas_call(kernel, out_shape=(jax.ShapeDtypeStruct((ROWS, FEAT), BF),...  102 us
    pallas_call x1, Pallas kernels, local(): pl.pallas_call(handover, out_shape=tuple((jax.ShapeDtypeStruct(r.shape, r...  2.59 us

profile of v4, /device:TPU:1, one launch (start us, length us, event | category | flops | bytes accessed | tf_op | source)
XLA Modules:
  0.0 105.4 jit_solution(9575457243767373906)
XLA Ops:
  0.6 102.1 %block.1 = (bf16[192,96]{1,0:T(8,128)(2,1)}, bf16[192,96]{1,0:T(8,128)(2,1)}, bf16[192,3072]{1,0:T(8,128)(2,1)}, bf16[768,768]{1,0:T(8,128)(2,1)}) custom-call(bf16[192,96]{1,0:T(8,128)(2,1)} %feat_hbm.1, bf16[192,96]{1,0:T(8,128)(2,1)} %cot_hbm.1, bf16[192,3072]{1,0:T(8,128)(2,1)} %w1_hbm.1, bf16[768,768]{1,0:T(8,128)(2,1)} %w2_hbm.1), custom_call_target="tpu_custom_call" | custom-call | flops 5435817984 | bytes 4718592 | tf_op jit(solution)/shard_map/block/pallas_call | solution.py:475
  102.8 2.6 %handover.1 = (bf16[192,96]{1,0:T(8,128)(2,1)}, bf16[192,96]{1,0:T(8,128)(2,1)}, bf16[192,3072]{1,0:T(8,128)(2,1)}, bf16[768,768]{1,0:T(8,128)(2,1)}) custom-call(bf16[192,96]{1,0:T(8,128)(2,1)} %get-tuple-element.8.refs_0_, bf16[192,96]{1,0:T(8,128)(2,1)} %get-tuple-element.9.refs_1_, bf16[192,3072]{1,0:T(8,128)(2,1)} %get-tuple-element.10.refs_2_, ...), custom_call_target="tpu_custom_call" | custom-call | tf_op jit(solution)/shard_map/handover/pallas_call | solution.py:511
